TPU v7x, 128 devices: a whole 4x4x4 slice. The times are simulated.
128 devices in a mesh: region: 128 (over y, z, x, core).
Axes of the slice: x: 4, y: 4, z: 4, core: 2. Of those that a mesh axis runs over, the one named last changes fastest.
Arguments:
- fields: bfloat16 [6144, 12, 32, 128], P('region'), may hold values from -6 to 6
- weights: bfloat16 [6144, 8, 128, 128], P('region'), may hold values from -0.1875 to 0.1875
- departures: int32 [6144, 8], P('region'), may hold values from 0 to 6143, as said below
Outputs:
- advected: bfloat16 [6144, 12, 32, 128], P('region')
Inputs may be any that keep to these rules, and one draw needn't show every extreme that they name: `departures`: blocks of device d are 48 * d to 48 * d + 47. Among the 384 slots of one device, the blocks of each other device are named by either no slot or exactly 2 slots; the two devices next to it (indices modulo 128) are always named, and on some device every other device is named.
All inputs are finite; a program needn't handle non-finite values.
Results may differ from a plain program's by a relative error of at most 0.001.
Values may be sent and summed in bfloat16 or wider, within the bound.
A program may use at most 192 MiB of HBM per device.

v0:
```python
import jax
import jax.numpy as jnp
from jax import lax
from jax.sharding import PartitionSpec as P

CAP = 2


def slot_ranks(owner_dev, peer_count):
    onehot = (owner_dev[:, None] == jnp.arange(peer_count, dtype=jnp.int32)[None, :]).astype(
        jnp.int32
    )
    before = jnp.cumsum(onehot, axis=0) - onehot
    return jnp.sum(before * onehot, axis=1)


def interpolate(source_pool, pick_ids, weights):
    per_dev = pick_ids.shape[0]
    slot_count = pick_ids.shape[1]
    tile_cols = weights.shape[2]
    tiles = weights.reshape(per_dev // 8, 8, slot_count, tile_cols, tile_cols)

    def one_group(items):
        ids_group, tile_group = items
        picked = source_pool[ids_group]
        result = jnp.einsum(
            "gsflk,gskc->gflc", picked, tile_group, preferred_element_type=jnp.float32
        )
        return result.astype(jnp.bfloat16)

    result = lax.map(one_group, (pick_ids.reshape(per_dev // 8, 8, slot_count), tiles))
    return result.reshape((per_dev,) + result.shape[2:])


def on_device(fields, weights, departures):
    peer_count = lax.axis_size("region")
    self_index = lax.axis_index("region")
    per_dev = fields.shape[0]
    slot_count = departures.shape[1]
    flat_ids = departures.reshape(-1)
    owner_dev = flat_ids // per_dev
    local_idx = flat_ids % per_dev
    slot_rank = slot_ranks(owner_dev, peer_count)
    is_remote = owner_dev != self_index
    dest_row = jnp.where(is_remote, owner_dev, peer_count)
    want_table = (
        jnp.zeros((peer_count, CAP), jnp.int32).at[dest_row, slot_rank].set(local_idx, mode="drop")
    )
    wanted = lax.all_to_all(want_table, "region", split_axis=0, concat_axis=0, tiled=True)
    pick_flat = jnp.where(is_remote, per_dev + owner_dev * CAP + slot_rank, local_idx)
    pick_ids = pick_flat.reshape(per_dev, slot_count)
    shape_tail = fields.shape[1:]
    outgoing = fields[wanted]
    incoming = lax.all_to_all(outgoing, "region", split_axis=0, concat_axis=0, tiled=True)
    source_pool = jnp.concatenate(
        [fields, incoming.reshape((peer_count * CAP,) + shape_tail)], axis=0
    )
    return interpolate(source_pool, pick_ids, weights)


def solution(mesh):
    in_specs = (P("region", None, None, None), P("region", None, None, None), P("region", None))
    out_specs = P("region", None, None, None)
    return jax.shard_map(
        on_device, mesh=mesh, in_specs=in_specs, out_specs=out_specs, check_vma=False
    )
```

profile of v0, /device:TPU:68, one launch (start us, length us, event | category | flops | bytes accessed | tf_op | source)
XLA Modules:
  0.0 592.5 jit_solution(17843740474132545879)
XLA Ops:
  0.0 0.7 broadcast_divide_fusion
  0.7 0.7 compare_and_fusion
  1.4 0.1 copy.25
  1.5 0.1 div.33
  1.6 0.1 div.32
  1.7 0.1 div.34
  1.8 0.1 copy.29
  1.9 0.1 and.37
  2.0 0.1 and.39
  2.1 0.1 copy.31
  2.2 0.2 fusion.12
  2.4 0.1 broadcast_add_fusion
  2.5 0.1 copy.24
  2.6 0.1 rem.41
  2.7 0.1 copy.23
  2.8 0.1 ne.93
  2.9 0.2 fusion.15
  3.2 18.0 %scatter_fusion = s32[128,2]{0,1:T(2,128)S(1)} fusion(s32[128,2]{0,1:T(2,128)S(1)} %broadcast.198, s32[384]{0:T(512)S(1)} %fusion.20, s32[384]{0:T(512)S(1)} %get-tuple-element.47), kind=kCustom, calls=%fused_computation.2 | custom fusion | bytes 7680 | tf_op jit(solution)/shard_map/scatter | solution.py:47
  21.2 0.1 copy.35
  21.3 16.1 %all_to_all.17 = s32[128,1,2]{2,1,0:T(1,128)S(1)} all-to-all(s32[128,1,2]{2,1,0:T(1,128)S(1)} %copy.35), channel_id=1, replica_groups=mesh['region'=128] {'region'}, dimensions={0} | all-to-all | bytes 2048 | tf_op jit(solution)/shard_map/all_to_all | solution.py:49
  37.4 0.1 reshape.215
  37.5 14.6 %gather_fusion.1 = bf16[256,12,32,128]{3,2,1,0:T(8,128)(2,1)} fusion(bf16[48,12,32,128]{3,2,1,0:T(8,128)(2,1)} %param.5, s32[1024]{0:T(1024)S(1)} %pad_clamp_fusion.1), kind=kCustom, calls=%fused_computation.1 | custom fusion | bytes 50332672 | tf_op jit(solution)/shard_map/gather | solution.py:53
  52.2 9.1 %all-to-all-start.1 = ((bf16[128,2,12,32,128]{4,3,2,1,0:T(8,128)(2,1)}), bf16[128,2,12,32,128]{4,3,2,1,0:T(8,128)(2,1)}, u32[]{:S(2)}, u32[]{:S(2)}) async-start(bf16[128,2,12,32,128]{4,3,2,1,0:T(8,128)(2,1)} %bitcast.86), calls=%async_computation.1 | async-start | bytes 50331648 | tf_op jit(solution)/shard_map/all_to_all | solution.py:54
  61.2 0.1 reduce_sum.14
  61.4 392.0 %all-to-all-done.1 = bf16[128,2,12,32,128]{4,3,2,1,0:T(8,128)(2,1)} async-done(((bf16[128,2,12,32,128]{4,3,2,1,0:T(8,128)(2,1)}), bf16[128,2,12,32,128]{4,3,2,1,0:T(8,128)(2,1)}, u32[]{:S(2)}, u32[]{:S(2)}) %all-to-all-start.1) | async-done | bytes 25165856 | tf_op jit(solution)/shard_map/all_to_all | solution.py:54
  453.4 21.0 %pad_maximum_fusion = bf16[304,12,32,128]{3,2,1,0:T(8,128)(2,1)} fusion(bf16[256,12,32,128]{3,2,1,0:T(8,128)(2,1)} %bitcast.17, bf16[48,12,32,128]{3,2,1,0:T(8,128)(2,1)} %param.5), kind=kLoop, calls=%fused_computation.12 | loop fusion | flops 14942208 | bytes 59768832 | tf_op jit(solution)/shard_map/concatenate | solution.py:55
  474.5 118.0 %while.10 = (s32[]{:T(128)}, bf16[6,8,12,32,128]{4,3,2,1,0:T(8,128)(2,1)}, s32[6,8,8]{2,1,0:T(8,128)S(1)}, bf16[304,12,32,128]{3,2,1,0:T(8,128)(2,1)}, bf16[6,8,8,128,128]{4,3,2,1,0:T(8,128)(2,1)}, /*index=5*/s32[]{:T(128)}) while((s32[]{:T(128)}, bf16[6,8,12,32,128]{4,3,2,1,0:T(8,128)(2,1)}, s32[6,8,8]{2,1,0:T(8,128)S(1)}, ...), condition=%wide.region_5.6_spmd, body=%wide.region_4.5_spmd.sunk | while | flops 805700800 | bytes 21764680 | solution.py:31
  474.5 0.1 reshape.237
  474.6 13.5 %gather_fusion = bf16[64,12,32,128]{3,2,1,0:T(8,128)(2,1)} fusion(bf16[304,12,32,128]{3,2,1,0:T(8,128)(2,1)} %get-tuple-element.95, s32[1024]{0:T(1024)S(1)} %pad_clamp_fusion.3), kind=kCustom, calls=%fused_computation.clone.1 | custom fusion | bytes 12583168 | tf_op jit(solution)/shard_map/while/body/eval_jaxpr/gather | solution.py:25
  488.1 6.1 %fusion.27 = bf16[6,8,12,32,128]{4,3,2,1,0:T(8,128)(2,1)} fusion(bf16[6,8,12,32,128]{4,3,2,1,0:T(8,128)(2,1)} %get-tuple-element.87, s32[]{:T(128)} %get-tuple-element.86, bf16[8,8,12,32,128]{4,3,2,1,0:T(8,128)(2,1)} %bitcast.85, bf16[6,8,8,128,128]{4,3,2,1,0:T(8,128)(2,1)} %get-tuple-element.96), kind=kOutput, calls=%fused_computation.8.clone.1 | convolution fusion | flops 805699584 | bytes 9176064 | tf_op jit(solution)/shard_map/while/body/eval_jaxpr/gsflk,gskc->gflc/dot_general | solution.py:26
  494.1 0.1 reshape.237
  494.2 13.5 %gather_fusion = bf16[64,12,32,128]{3,2,1,0:T(8,128)(2,1)} fusion(bf16[304,12,32,128]{3,2,1,0:T(8,128)(2,1)} %get-tuple-element.95, s32[1024]{0:T(1024)S(1)} %pad_clamp_fusion.3), kind=kCustom, calls=%fused_computation.clone.1 | custom fusion | bytes 12583168 | tf_op jit(solution)/shard_map/while/body/eval_jaxpr/gather | solution.py:25
  507.7 6.1 %fusion.27 = bf16[6,8,12,32,128]{4,3,2,1,0:T(8,128)(2,1)} fusion(bf16[6,8,12,32,128]{4,3,2,1,0:T(8,128)(2,1)} %get-tuple-element.87, s32[]{:T(128)} %get-tuple-element.86, bf16[8,8,12,32,128]{4,3,2,1,0:T(8,128)(2,1)} %bitcast.85, bf16[6,8,8,128,128]{4,3,2,1,0:T(8,128)(2,1)} %get-tuple-element.96), kind=kOutput, calls=%fused_computation.8.clone.1 | convolution fusion | flops 805699584 | bytes 9176064 | tf_op jit(solution)/shard_map/while/body/eval_jaxpr/gsflk,gskc->gflc/dot_general | solution.py:26
  513.8 0.1 reshape.237
  513.9 13.5 %gather_fusion = bf16[64,12,32,128]{3,2,1,0:T(8,128)(2,1)} fusion(bf16[304,12,32,128]{3,2,1,0:T(8,128)(2,1)} %get-tuple-element.95, s32[1024]{0:T(1024)S(1)} %pad_clamp_fusion.3), kind=kCustom, calls=%fused_computation.clone.1 | custom fusion | bytes 12583168 | tf_op jit(solution)/shard_map/while/body/eval_jaxpr/gather | solution.py:25
  527.4 6.1 %fusion.27 = bf16[6,8,12,32,128]{4,3,2,1,0:T(8,128)(2,1)} fusion(bf16[6,8,12,32,128]{4,3,2,1,0:T(8,128)(2,1)} %get-tuple-element.87, s32[]{:T(128)} %get-tuple-element.86, bf16[8,8,12,32,128]{4,3,2,1,0:T(8,128)(2,1)} %bitcast.85, bf16[6,8,8,128,128]{4,3,2,1,0:T(8,128)(2,1)} %get-tuple-element.96), kind=kOutput, calls=%fused_computation.8.clone.1 | convolution fusion | flops 805699584 | bytes 9176064 | tf_op jit(solution)/shard_map/while/body/eval_jaxpr/gsflk,gskc->gflc/dot_general | solution.py:26
  533.5 0.1 reshape.237
  533.6 13.5 %gather_fusion = bf16[64,12,32,128]{3,2,1,0:T(8,128)(2,1)} fusion(bf16[304,12,32,128]{3,2,1,0:T(8,128)(2,1)} %get-tuple-element.95, s32[1024]{0:T(1024)S(1)} %pad_clamp_fusion.3), kind=kCustom, calls=%fused_computation.clone.1 | custom fusion | bytes 12583168 | tf_op jit(solution)/shard_map/while/body/eval_jaxpr/gather | solution.py:25
  547.0 6.1 %fusion.27 = bf16[6,8,12,32,128]{4,3,2,1,0:T(8,128)(2,1)} fusion(bf16[6,8,12,32,128]{4,3,2,1,0:T(8,128)(2,1)} %get-tuple-element.87, s32[]{:T(128)} %get-tuple-element.86, bf16[8,8,12,32,128]{4,3,2,1,0:T(8,128)(2,1)} %bitcast.85, bf16[6,8,8,128,128]{4,3,2,1,0:T(8,128)(2,1)} %get-tuple-element.96), kind=kOutput, calls=%fused_computation.8.clone.1 | convolution fusion | flops 805699584 | bytes 9176064 | tf_op jit(solution)/shard_map/while/body/eval_jaxpr/gsflk,gskc->gflc/dot_general | solution.py:26
  553.1 0.1 reshape.237
  553.2 13.5 %gather_fusion = bf16[64,12,32,128]{3,2,1,0:T(8,128)(2,1)} fusion(bf16[304,12,32,128]{3,2,1,0:T(8,128)(2,1)} %get-tuple-element.95, s32[1024]{0:T(1024)S(1)} %pad_clamp_fusion.3), kind=kCustom, calls=%fused_computation.clone.1 | custom fusion | bytes 12583168 | tf_op jit(solution)/shard_map/while/body/eval_jaxpr/gather | solution.py:25
  566.7 6.1 %fusion.27 = bf16[6,8,12,32,128]{4,3,2,1,0:T(8,128)(2,1)} fusion(bf16[6,8,12,32,128]{4,3,2,1,0:T(8,128)(2,1)} %get-tuple-element.87, s32[]{:T(128)} %get-tuple-element.86, bf16[8,8,12,32,128]{4,3,2,1,0:T(8,128)(2,1)} %bitcast.85, bf16[6,8,8,128,128]{4,3,2,1,0:T(8,128)(2,1)} %get-tuple-element.96), kind=kOutput, calls=%fused_computation.8.clone.1 | convolution fusion | flops 805699584 | bytes 9176064 | tf_op jit(solution)/shard_map/while/body/eval_jaxpr/gsflk,gskc->gflc/dot_general | solution.py:26
  572.8 0.1 reshape.237
  572.9 13.5 %gather_fusion = bf16[64,12,32,128]{3,2,1,0:T(8,128)(2,1)} fusion(bf16[304,12,32,128]{3,2,1,0:T(8,128)(2,1)} %get-tuple-element.95, s32[1024]{0:T(1024)S(1)} %pad_clamp_fusion.3), kind=kCustom, calls=%fused_computation.clone.1 | custom fusion | bytes 12583168 | tf_op jit(solution)/shard_map/while/body/eval_jaxpr/gather | solution.py:25
  586.4 6.1 %fusion.27 = bf16[6,8,12,32,128]{4,3,2,1,0:T(8,128)(2,1)} fusion(bf16[6,8,12,32,128]{4,3,2,1,0:T(8,128)(2,1)} %get-tuple-element.87, s32[]{:T(128)} %get-tuple-element.86, bf16[8,8,12,32,128]{4,3,2,1,0:T(8,128)(2,1)} %bitcast.85, bf16[6,8,8,128,128]{4,3,2,1,0:T(8,128)(2,1)} %get-tuple-element.96), kind=kOutput, calls=%fused_computation.8.clone.1 | convolution fusion | flops 805699584 | bytes 9176064 | tf_op jit(solution)/shard_map/while/body/eval_jaxpr/gsflk,gskc->gflc/dot_general | solution.py:26
  (23 shorter events, 0.2 us)
Async XLA Ops:
  52.2 401.2 %all-to-all-start.1 = ((bf16[128,2,12,32,128]{4,3,2,1,0:T(8,128)(2,1)}), bf16[128,2,12,32,128]{4,3,2,1,0:T(8,128)(2,1)}, u32[]{:S(2)}, u32[]{:S(2)}) async-start(bf16[128,2,12,32,128]{4,3,2,1,0:T(8,128)(2,1)} %bitcast.86), calls=%async_computation.1 | async-start | bytes 50331648 | tf_op jit(solution)/shard_map/all_to_all | solution.py:54
where the time goes:
time: 593 us; the launch traced here: 592 us
  waiting for transfers between devices  392 us (66%)
  local copies, waits for them, and re-layouts  116 us (20%)
  matrix products  36.5 us (6%)
  other arithmetic  23.1 us (4%)
  blocking collectives  16.1 us (3%)
  starting transfers between devices  9.06 us (2%)
    all_to_all x1, waiting for transfers between devices, on_device(): lax.all_to_all(outgoing, 'region', split_axis=0, concat_axis=0, tiled=True)  392 us
    gather x6, local copies, waits for them, and re-layouts, one_group(): picked = source_pool[ids_group]  80.9 us
    dot_general x6, matrix products, one_group(): jnp.einsum('gsflk,gskc->gflc', picked, tile_group, preferred_element_type...  36.5 us
    concatenate x1, other arithmetic, on_device(): jnp.concatenate([fields, incoming.reshape((peer_count * CAP,) + shape_tai...  21 us
    scatter x1, local copies, waits for them, and re-layouts, on_device(): jnp.zeros((peer_count, CAP), jnp.int32).at[dest_row, slot_rank]  18 us
    all_to_all x1, blocking collectives, on_device(): lax.all_to_all(want_table, 'region', split_axis=0, concat_axis=0, tiled=T...  16.1 us
    gather x1, local copies, waits for them, and re-layouts, on_device(): outgoing = fields[wanted]  14.6 us
  transfers between devices with their start and end apart: 1, of which 1 were waited for; matrix products, arithmetic and copies ran while one was open for 0% of the time, Pallas kernels for 0%

commit v1 on v0

v1 whole, which is shorter than its diff:
```python
import functools

import jax
import jax.numpy as jnp
from jax import lax
from jax.experimental import pallas as pl
from jax.experimental.pallas import tpu as pltpu
from jax.sharding import PartitionSpec as P

MESH = pl.DeviceIdType.MESH
SIDE = 4
PEERS = 128
GROUPS = 3
PHASES = 2
PICKS = 2
REMOTE = PEERS * PICKS


def coords(device):
    return [device // 32, (device // 8) % 4, (device // 2) % 4, device % 2]


def index_of(position):
    y, z, x, core = position
    return ((y * 4 + z) * 4 + x) * 2 + core


def shifted(position, axis, steps, core_flip=0):
    moved = list(position)
    moved[axis] = (moved[axis] + steps) % SIDE
    if core_flip:
        moved[3] = 1 - moved[3]
    return index_of(moved)


def exchange_kernel(wants, fields, pool, landing, *scratch):
    count = GROUPS * PHASES
    near = [scratch[i * SIDE : (i + 1) * SIDE] for i in range(count)]
    bundle = scratch[count * SIDE : count * SIDE + count]
    own_sem, a_send, a_recv, b_send, b_recv, c_send, c_recv, keep_sem = scratch[count * SIDE + count :]
    blocks = fields.shape[0]
    half = blocks // 2
    rows = fields.shape[2] // PHASES
    me = lax.axis_index("region")
    here = coords(me)

    peers = [shifted(here, axis, steps, flip) for axis in range(3) for steps in (1, 2, 3) for flip in (0, 1)]
    peers.append(shifted(here, 0, 0, 1))
    barrier = pltpu.get_barrier_semaphore()
    for peer in peers:
        pl.semaphore_signal(barrier, inc=1, device_id=(peer,), device_id_type=MESH)
    pl.semaphore_wait(barrier, len(peers))

    def send(src, dst, send_sem, recv_sem, device):
        copy = pltpu.make_async_remote_copy(
            src_ref=src, dst_ref=dst, send_sem=send_sem, recv_sem=recv_sem, device_id=(device,), device_id_type=MESH
        )
        copy.start()
        return copy

    low, high = pl.ds(0, half), pl.ds(half, half)

    def start_gather(k):
        phase, group = divmod(k, GROUPS)
        part = pl.ds(phase * rows, rows)
        up, down = shifted(here, group, 1), shifted(here, group, 3)
        own = pltpu.make_async_copy(fields.at[:, group, part, :], near[k][0], own_sem.at[k])
        own.start()
        plan = (
            (low, near[k][3], up),
            (high, near[k][1], down),
            (high, near[k][3], up),
            (low, near[k][1], down),
        )
        copies = [
            send(fields.at[span, group, part, :], dst.at[span], a_send.at[k, i], a_recv.at[k, i], device)
            for i, (span, dst, device) in enumerate(plan)
        ]
        return own, copies

    def relay_gather(k, copies):
        group = k % GROUPS
        up, down = shifted(here, group, 1), shifted(here, group, 3)
        copies[0].wait_recv()
        copies.append(send(near[k][3].at[low], near[k][2].at[low], a_send.at[k, 4], a_recv.at[k, 4], up))
        copies[1].wait_recv()
        copies.append(send(near[k][1].at[high], near[k][2].at[high], a_send.at[k, 5], a_recv.at[k, 5], down))

    def pick(k, ja, tb):
        group = k % GROUPS
        axis_a, axis_b, axis_c = group, (group + 1) % 3, (group + 2) % 3
        source = list(here)
        source[axis_a] = (source[axis_a] + ja) % SIDE
        column = index_of(source) * PICKS

        def one(t, carry):
            target = list(here)
            target[axis_b] = (target[axis_b] + tb) % SIDE
            target[axis_c] = (target[axis_c] + t // 2) % SIDE
            target[3] = (target[3] + t) % 2
            row = index_of(target)
            for r in range(PICKS):
                bundle[k][tb, t, ja, r] = near[k][ja][wants[row, column + r]]
            return carry

        lax.fori_loop(0, 2 * SIDE, one, 0)

    def finish_gather(k, own, copies):
        own.wait()
        for tb in range(SIDE):
            pick(k, 0, tb)
        copies[3].wait_recv()
        for tb in range(SIDE):
            pick(k, 1, tb)
        copies[2].wait_recv()
        for tb in range(SIDE):
            pick(k, 3, tb)
        copies[4].wait_recv()
        copies[5].wait_recv()

    def last_pick_and_send(k):
        phase, group = divmod(k, GROUPS)
        axis_b = (group + 1) % 3
        copies = {}
        for tb in (2, 1, 3, 0):
            pick(k, 2, tb)
            if tb:
                jb = SIDE - tb
                copies[jb] = send(
                    bundle[k].at[tb],
                    landing.at[phase, group, jb - 1],
                    b_send.at[k, tb - 1],
                    b_recv.at[k, jb - 1],
                    shifted(here, axis_b, tb),
                )
        return copies

    def home(k, jb, jc, jcore):
        phase, group = divmod(k, GROUPS)
        place = [None] * 3
        place[group] = slice(None)
        place[(group + 1) % 3] = jb
        place[(group + 2) % 3] = jc
        return pool.at[(phase, group) + tuple(place) + (jcore,)]

    def send_on(k, jb):
        phase, group = divmod(k, GROUPS)
        axis_c = (group + 2) % 3
        for t in (4, 5, 2, 3, 6, 7, 1, 0):
            tc, flip = divmod(t, 2)
            src = bundle[k].at[0, t] if jb == 0 else landing.at[phase, group, jb - 1, t]
            dst = home(k, jb, (SIDE - tc) % SIDE, flip)
            if t == 0:
                pltpu.make_async_copy(src, dst, keep_sem.at[k, jb]).start()
            else:
                send(src, dst, c_send.at[k, t - 1], c_recv.at[k, (SIDE - tc) % SIDE], shifted(here, axis_c, tc, flip))

    def column(k, jc, cores):
        phase, group = divmod(k, GROUPS)
        place = [slice(None)] * 3
        place[(group + 2) % 3] = jc
        return pool.at[(phase, group) + tuple(place) + (cores,)]

    def drain(k):
        for jc in range(SIDE):
            ref = column(k, jc, slice(None) if jc else 1)
            pltpu.make_async_copy(ref, ref, c_recv.at[k, jc]).wait()
        for t in range(1, 2 * SIDE):
            ref = column(k, 0, 0)
            pltpu.make_async_copy(ref, ref, c_send.at[k, t - 1]).wait()
        for jb in range(SIDE):
            ref = home(k, jb, 0, 0)
            pltpu.make_async_copy(ref, ref, keep_sem.at[k, jb]).wait()

    gathered, along = {}, {}
    first = range(GROUPS)
    for k in first:
        gathered[k] = start_gather(k)
    for phase in range(PHASES):
        ks = range(phase * GROUPS, (phase + 1) * GROUPS)
        for k in ks:
            relay_gather(k, gathered[k][1])
        for k in ks:
            finish_gather(k, *gathered[k])
            if phase + 1 < PHASES:
                gathered[k + GROUPS] = start_gather(k + GROUPS)
        for k in ks:
            along[k] = last_pick_and_send(k)
            send_on(k, 0)
    for k in range(count):
        for jb in (1, 3, 2):
            along[k][jb].wait_recv()
            send_on(k, jb)
    for k in range(count):
        drain(k)
        for copy in gathered[k][1]:
            copy.wait_send()
        for copy in along[k].values():
            copy.wait_send()


def exchange(wants, fields):
    blocks, _, group_rows, cols = fields.shape
    rows = group_rows // PHASES
    count = GROUPS * PHASES
    kind = fields.dtype
    dma = pltpu.SemaphoreType.DMA
    any_spec = pl.BlockSpec(memory_space=pl.ANY)
    scratch = [pltpu.VMEM((blocks, rows, cols), kind) for _ in range(count * SIDE)]
    scratch += [pltpu.VMEM((SIDE, 2 * SIDE, SIDE, PICKS, rows, cols), kind) for _ in range(count)]
    scratch += [
        dma((count,)),
        dma((count, 6)),
        dma((count, 6)),
        dma((count, 3)),
        dma((count, 3)),
        dma((count, 7)),
        dma((count, SIDE)),
        dma((count, SIDE)),
    ]
    pool, _ = pl.pallas_call(
        exchange_kernel,
        out_shape=(
            jax.ShapeDtypeStruct((PHASES, GROUPS, SIDE, SIDE, SIDE, 2, PICKS, rows, cols), kind),
            jax.ShapeDtypeStruct((PHASES, GROUPS, SIDE - 1, 2 * SIDE, SIDE, PICKS, rows, cols), kind),
        ),
        in_specs=[pl.BlockSpec(memory_space=pltpu.SMEM), any_spec],
        out_specs=(any_spec, any_spec),
        scratch_shapes=scratch,
        compiler_params=pltpu.CompilerParams(
            collective_id=0, has_side_effects=True, vmem_limit_bytes=56 * 1024 * 1024
        ),
    )(wants, fields)
    return pool.reshape(PHASES, GROUPS, REMOTE, rows, cols)


def interpolate_kernel(picks, pool, fields, weights, out):
    slots = weights.shape[1]
    cols = weights.shape[2]

    def one(b, carry):
        total = None
        for s in range(0, slots, 2):
            pair = []
            for i in (s, s + 1):
                pick = picks[b, i]
                away = pool[0, 0, jnp.minimum(pick, REMOTE - 1)]
                local = fields[jnp.maximum(pick - REMOTE, 0), 0, 0]
                pair.append(jnp.where(pick < REMOTE, away, local))
            left = jnp.concatenate(pair, axis=1)
            right = weights[b, s : s + 2].reshape(2 * cols, cols)
            part = jnp.dot(left, right, preferred_element_type=jnp.float32)
            total = part if total is None else total + part
        out[b, 0, 0] = total.astype(out.dtype)
        return carry

    lax.fori_loop(0, weights.shape[0], one, 0)


def interpolate(picks, pool, fields, weights):
    blocks, _, group_rows, cols = fields.shape
    rows = group_rows // PHASES
    split = fields.reshape(blocks, GROUPS, PHASES, rows, cols)
    part = pl.BlockSpec((blocks, 1, 1, rows, cols), lambda p, g: (0, g, p, 0, 0))
    return pl.pallas_call(
        interpolate_kernel,
        grid=(PHASES, GROUPS),
        out_shape=jax.ShapeDtypeStruct(split.shape, fields.dtype),
        in_specs=[
            pl.BlockSpec(memory_space=pltpu.SMEM),
            pl.BlockSpec((1, 1, REMOTE, rows, cols), lambda p, g: (p, g, 0, 0, 0)),
            part,
            pl.BlockSpec(weights.shape, lambda p, g: (0, 0, 0, 0), pipeline_mode=pl.Buffered(1)),
        ],
        out_specs=part,
        compiler_params=pltpu.CompilerParams(vmem_limit_bytes=56 * 1024 * 1024),
    )(picks, pool, split, weights)


def tables(departures, blocks):
    me = lax.axis_index("region")
    flat = departures.reshape(-1)
    owner = flat // blocks
    local = flat % blocks
    key = jnp.arange(flat.shape[0], dtype=jnp.int32) * 64 + local
    named = owner[None, :] == jnp.arange(PEERS, dtype=jnp.int32)[:, None]
    first = jnp.min(jnp.where(named, key[None, :], 1 << 30), axis=1)
    last = jnp.max(jnp.where(named, key[None, :], 0), axis=1)
    wants = jnp.stack([jnp.where(first < (1 << 30), first, 0) % 64, last % 64], axis=1)
    is_first = jnp.any(named & (key[None, :] == first[:, None]), axis=0)
    rank = jnp.where(is_first, 0, 1)
    there, here = coords(owner), coords(me)
    offset = [(there[i] - here[i]) % SIDE for i in range(3)] + [(there[3] - here[3]) % 2]
    picks = jnp.where(owner == me, REMOTE + local, index_of(offset) * PICKS + rank)
    return wants, picks.reshape(departures.shape)


def on_device(fields, weights, departures):
    blocks, field_count, levels, cols = fields.shape
    grouped = fields.reshape(blocks, GROUPS, field_count // GROUPS * levels, cols)
    wants, picks = tables(departures, blocks)
    wants = lax.all_gather(wants.reshape(-1), "region", axis=0)
    pool = exchange(wants, grouped)
    return interpolate(picks, pool, grouped, weights).reshape(fields.shape)


def solution(mesh):
    in_specs = (P("region", None, None, None), P("region", None, None, None), P("region", None))
    out_specs = P("region", None, None, None)
    return jax.shard_map(on_device, mesh=mesh, in_specs=in_specs, out_specs=out_specs, check_vma=False)
```

time: 593 us -> 352 us (0.59)
  the two profiles are of different devices: /device:TPU:68 before, /device:TPU:1 now
where the time goes in v1:
time: 352 us
  Pallas kernels  310 us (88%)
  blocking collectives  38.7 us (11%)
    pallas_call x1, Pallas kernels, exchange(): pl.pallas_call(exchange_kernel, out_shape=(jax.ShapeDtypeStruct((PHASES,...  250 us
    pallas_call x1, Pallas kernels, interpolate(): pl.pallas_call(interpolate_kernel, grid=(PHASES, GROUPS), out_shape=jax.S...  59.8 us
    all_gather x1, blocking collectives, on_device(): wants = lax.all_gather(wants.reshape(-1), 'region', axis=0)  38.7 us

profile of v1, /device:TPU:1, one launch (start us, length us, event | category | flops | bytes accessed | tf_op | source)
XLA Modules:
  0.0 351.9 jit_solution(11267244332222251215)
XLA Ops:
  0.0 0.8 copy.17
  0.8 0.1 ne.212
  0.9 0.1 div.82
  1.0 0.1 rem.330
  1.1 0.1 select_reduce_fusion
  1.2 0.1 fusion.1
  1.4 0.1 select_n.173
  1.5 0.7 fusion.3.picks
  2.2 0.1 copy.20
  2.3 0.1 reshape.136
  2.5 38.7 %all-gather = s32[128,1,256]{2,1,0:T(1,128)S(1)} all-gather(s32[1,1,256]{2,1,0:T(1,128)S(1)} %reshape.136), channel_id=1, replica_groups=mesh['region'=128] {'region'}, dimensions={0}, use_global_device_ids=true | all-gather | bytes 132096 | tf_op jit(solution)/shard_map/all_gather | solution.py:302
  41.2 0.7 copy.23
  41.9 250.2 %shard_map.37 = (bf16[2,3,4,4,4,2,2,64,128]{8,7,6,5,4,3,2,1,0:T(8,128)(2,1)}, bf16[2,3,3,8,4,2,64,128]{7,6,5,4,3,2,1,0:T(8,128)(2,1)}) custom-call(s32[128,256]{1,0:T(8,128)} %bitcast.14, bf16[48,3,128,128]{3,2,1,0:T(8,128)(2,1)} %bitcast.12), custom_call_target="tpu_custom_call" | custom-call | tf_op jit(solution)/shard_map/pallas_call | solution.py:221
  292.0 59.8 %shard_map.38 = bf16[48,3,2,64,128]{4,3,2,1,0:T(8,128)(2,1)} custom-call(s32[48,8]{1,0:T(8,128)} %fusion.3.picks, bf16[2,3,256,64,128]{4,3,2,1,0:T(8,128)(2,1)} %bitcast.11, bf16[48,3,2,64,128]{4,3,2,1,0:T(8,128)(2,1)} %bitcast.13, bf16[48,8,128,128]{3,2,1,0:T(8,128)(2,1)} %weights.1), custom_call_target="tpu_custom_call" | custom-call | tf_op jit(solution)/shard_map/pallas_call | solution.py:265
  (6 shorter events, 0.1 us)

commit v2 on v1

v2 whole, which is shorter than its diff:
```python
import jax
import jax.numpy as jnp
from jax import lax
from jax.experimental import pallas as pl
from jax.experimental.pallas import tpu as pltpu
from jax.sharding import PartitionSpec as P

MESH = pl.DeviceIdType.MESH
SIDE = 4
PEERS = 128
GROUPS = 3
PHASES = 2
PICKS = 2
REMOTE = PEERS * PICKS
CHUNK = 4


def coords(device):
    return [device // 32, (device // 8) % 4, (device // 2) % 4, device % 2]


def index_of(position):
    y, z, x, core = position
    return ((y * 4 + z) * 4 + x) * 2 + core


def shifted(position, axis, steps, core_flip=0):
    moved = list(position)
    moved[axis] = (moved[axis] + steps) % SIDE
    if core_flip:
        moved[3] = 1 - moved[3]
    return index_of(moved)


def axes_of(group):
    return group, (group + 1) % 3, (group + 2) % 3


def fused_kernel(picks, own_wants, fields, weights, out, landing, want_rows, *scratch):
    count = GROUPS * PHASES
    near = [scratch[i * SIDE : (i + 1) * SIDE] for i in range(count)]
    scratch = scratch[count * SIDE :]
    bundle, scratch = scratch[:GROUPS], scratch[GROUPS:]
    pool, scratch = scratch[:count], scratch[count:]
    wants, tiles, result, *sems = scratch
    meta_send, meta_recv, own_sem, a_send, a_recv, b_send, b_recv, c_first, c_send, c_recv, keep_sem, w_sem, o_sem = sems
    blocks, _, group_rows, _ = fields.shape
    half = blocks // 2
    rows = group_rows // PHASES
    here = coords(lax.axis_index("region"))

    def send(src, dst, send_sem, recv_sem, device):
        copy = pltpu.make_async_remote_copy(
            src_ref=src, dst_ref=dst, send_sem=send_sem, recv_sem=recv_sem, device_id=(device,), device_id_type=MESH
        )
        copy.start()
        return copy

    def await_bytes(ref, sem):
        pltpu.make_async_copy(ref, ref, sem).wait()

    def keep(src, dst, sem):
        copy = pltpu.make_async_copy(src, dst, sem)
        copy.start()
        return copy

    def fetch_tiles(chunk, slot):
        return keep(weights.at[pl.ds(chunk * CHUNK, CHUNK)], tiles.at[slot], w_sem.at[slot])

    fetch_tiles(0, 0)
    own_copies = [
        keep(fields.at[:, k % GROUPS, pl.ds(k // GROUPS * rows, rows), :], near[k][0], own_sem.at[k])
        for k in range(count)
    ]
    own_row = keep(own_wants, want_rows.at[0], meta_send.at[13])

    peers = [shifted(here, axis, steps, flip) for axis in range(3) for steps in (1, 2, 3) for flip in (0, 1)]
    peers.append(shifted(here, 0, 0, 1))
    barrier = pltpu.get_barrier_semaphore()
    for peer in peers:
        pl.semaphore_signal(barrier, inc=1, device_id=(peer,), device_id_type=MESH)
    pl.semaphore_wait(barrier, len(peers))

    def send_wants_z():
        copies = []
        for steps in range(SIDE):
            for flip in (0, 1):
                if steps or flip:
                    row = (SIDE - steps) % SIDE * 2 + flip
                    peer = shifted(here, 1, steps, flip)
                    copies.append(
                        send(own_wants, want_rows.at[row], meta_send.at[len(copies)], meta_recv.at[0], peer)
                    )
        return copies

    def send_wants(axis, first_sem, known, stage):
        return [
            send(
                want_rows.at[pl.ds(0, known)],
                want_rows.at[pl.ds((SIDE - steps) * known, known)],
                meta_send.at[first_sem + steps - 1],
                meta_recv.at[stage],
                shifted(here, axis, steps),
            )
            for steps in (1, 2, 3)
        ]

    low, high = pl.ds(0, half), pl.ds(half, half)

    def start_gather(k):
        phase, group = divmod(k, GROUPS)
        part = pl.ds(phase * rows, rows)
        up, down = shifted(here, group, 1), shifted(here, group, 3)
        plan = (
            (low, near[k][3], up),
            (high, near[k][1], down),
            (high, near[k][3], up),
            (low, near[k][1], down),
        )
        return [
            send(fields.at[span, group, part, :], dst.at[span], a_send.at[k, i], a_recv.at[k, i], device)
            for i, (span, dst, device) in enumerate(plan)
        ]

    def relay_gather(k, copies):
        group = k % GROUPS
        up, down = shifted(here, group, 1), shifted(here, group, 3)
        copies[0].wait_recv()
        copies.append(send(near[k][3].at[low], near[k][2].at[low], a_send.at[k, 4], a_recv.at[k, 4], up))
        copies[1].wait_recv()
        copies.append(send(near[k][1].at[high], near[k][2].at[high], a_send.at[k, 5], a_recv.at[k, 5], down))

    def pick(k, ja, tb):
        group = k % GROUPS
        axis_a, axis_b, axis_c = axes_of(group)
        source = list(here)
        source[axis_a] = (source[axis_a] + ja) % SIDE
        column = index_of(source)

        def one(t, carry):
            away = [0, 0, 0]
            away[axis_b] = tb
            away[axis_c] = t // 2
            row = ((away[0] * 4 + away[2]) * 4 + away[1]) * 2 + t % 2
            for r in range(PICKS):
                bundle[group][tb, t, ja * PICKS + r] = near[k][ja][wants[row, r, column]]
            return carry

        lax.fori_loop(0, 2 * SIDE, one, 0)

    def send_bundle(k, tb):
        jb = SIDE - tb
        _, axis_b, _ = axes_of(k % GROUPS)
        return send(
            bundle[k % GROUPS].at[tb],
            landing.at[k, jb - 1],
            b_send.at[k, tb - 1],
            b_recv.at[k, jb - 1],
            shifted(here, axis_b, tb),
        )

    def send_on(k, jb):
        group = k % GROUPS
        _, _, axis_c = axes_of(group)
        for t in (4, 5, 2, 3, 6, 7, 1, 0):
            tc, flip = divmod(t, 2)
            src = bundle[group].at[0, t] if jb == 0 else landing.at[k, jb - 1, t]
            jc = (SIDE - tc) % SIDE
            dst = pool[k].at[pl.ds(((jb * SIDE + jc) * 2 + flip) * 8, 8)]
            if t == 0:
                keep(src, dst, keep_sem.at[k, jb])
            else:
                sent = c_send.at[k, t - 1] if jb else c_first.at[k, t - 1]
                send(src, dst, sent, c_recv.at[k, jc], shifted(here, axis_c, tc, flip))

    def await_kept(k, jb):
        await_bytes(pool[k].at[pl.ds(0, 8)], keep_sem.at[k, jb])

    def free_bundle(k, along):
        for copy in along.values():
            copy.wait_send()
        for t in range(1, 2 * SIDE):
            await_bytes(pool[k].at[pl.ds(0, 8)], c_first.at[k, t - 1])
        await_kept(k, 0)

    def await_pool(k):
        for jc in range(SIDE):
            await_bytes(pool[k].at[pl.ds(0, 64 if jc else 32)], c_recv.at[k, jc])
        for jb in range(1, SIDE):
            await_kept(k, jb)

    def interpolate(phase):
        chunks = blocks // CHUNK
        part = pl.ds(phase * rows, rows)

        def write_back(chunk, slot):
            span = pl.ds(chunk * CHUNK, CHUNK)
            return pltpu.make_async_copy(result.at[slot], out.at[span, :, part, :], o_sem.at[slot])

        def source(b, s):
            parts = []
            for group in range(GROUPS):
                k = phase * GROUPS + group
                at = picks[group, b, s]
                away = pool[k][jnp.minimum(at, REMOTE - 1)]
                local = near[k][0][jnp.maximum(at - REMOTE, 0)]
                parts.append(jnp.where(at < REMOTE, away, local))
            return jnp.concatenate(parts, axis=0)

        def one(chunk, carry):
            slot = chunk % 2
            await_bytes(tiles.at[slot], w_sem.at[slot])

            @pl.when(chunk + 1 < chunks)
            def _():
                fetch_tiles(chunk + 1, 1 - slot)

            @pl.when(chunk >= 2)
            def _():
                write_back(chunk - 2, slot).wait()

            for i in range(CHUNK):
                b = chunk * CHUNK + i
                total = None
                for s in range(0, weights.shape[1], 2):
                    left = jnp.concatenate([source(b, s), source(b, s + 1)], axis=1)
                    right = tiles[slot, i, s : s + 2].reshape(2 * weights.shape[2], weights.shape[3])
                    dot = jnp.dot(left, right, preferred_element_type=jnp.float32)
                    total = dot if total is None else total + dot
                total = total.astype(out.dtype)
                for group in range(GROUPS):
                    result[slot, i, group] = total[group * rows : (group + 1) * rows]
            write_back(chunk, slot).start()
            return carry

        lax.fori_loop(0, chunks, one, 0)
        for chunk in (chunks - 2, chunks - 1):
            write_back(chunk, chunk % 2).wait()

    gathered, along = {}, {}
    meta = send_wants_z()
    for k in range(GROUPS):
        gathered[k] = start_gather(k)
    own_row.wait()
    await_bytes(want_rows.at[pl.ds(0, 7)], meta_recv.at[0])
    meta += send_wants(2, 7, 8, 1)
    for k in range(GROUPS):
        relay_gather(k, gathered[k])
    await_bytes(want_rows.at[pl.ds(0, 24)], meta_recv.at[1])
    meta += send_wants(0, 10, 32, 2)
    for copy in own_copies:
        copy.wait()
    await_bytes(want_rows.at[pl.ds(0, 96)], meta_recv.at[2])
    table = keep(want_rows, wants, meta_send.at[13])
    table.wait()

    for phase in range(PHASES):
        ks = range(phase * GROUPS, (phase + 1) * GROUPS)
        for k in ks:
            if phase:
                free_bundle(k - GROUPS, along[k - GROUPS])
            for tb in range(SIDE):
                pick(k, 0, tb)
        for k in ks:
            gathered[k][3].wait_recv()
            for tb in range(SIDE):
                pick(k, 1, tb)
            gathered[k][2].wait_recv()
            for tb in range(SIDE):
                pick(k, 3, tb)
        for k in ks:
            gathered[k][4].wait_recv()
            gathered[k][5].wait_recv()
            if phase + 1 < PHASES:
                gathered[k + GROUPS] = start_gather(k + GROUPS)
        for k in ks:
            along[k] = {}
            for tb in (2, 1, 3, 0):
                pick(k, 2, tb)
                if tb:
                    along[k][SIDE - tb] = send_bundle(k, tb)
            send_on(k, 0)
        if phase + 1 < PHASES:
            for k in ks:
                relay_gather(k + GROUPS, gathered[k + GROUPS])
        for jb in (1, 3, 2):
            for k in ks:
                along[k][jb].wait_recv()
                send_on(k, jb)

    for phase in range(PHASES):
        for k in range(phase * GROUPS, (phase + 1) * GROUPS):
            await_pool(k)
            if phase == PHASES - 1:
                free_bundle(k, along[k])
        if phase:
            fetch_tiles(0, 0)
        interpolate(phase)

    for copy in meta:
        copy.wait_send()
    for k in range(count):
        for copy in gathered[k]:
            copy.wait_send()
        for t in range(1, 2 * SIDE):
            await_bytes(pool[k].at[pl.ds(0, 24)], c_send.at[k, t - 1])


def fused(picks, wants, fields, weights):
    blocks, _, group_rows, cols = fields.shape
    rows = group_rows // PHASES
    count = GROUPS * PHASES
    kind = fields.dtype
    dma = pltpu.SemaphoreType.DMA
    any_spec = pl.BlockSpec(memory_space=pl.ANY)
    scratch = [pltpu.VMEM((blocks, rows, cols), kind) for _ in range(count * SIDE)]
    scratch += [pltpu.VMEM((SIDE, 2 * SIDE, SIDE * PICKS, rows, cols), kind) for _ in range(GROUPS)]
    scratch += [pltpu.VMEM((REMOTE, rows, cols), kind) for _ in range(count)]
    scratch += [
        pltpu.SMEM((PEERS, PICKS, PEERS), jnp.int32),
        pltpu.VMEM((2, CHUNK) + weights.shape[1:], kind),
        pltpu.VMEM((2, CHUNK, GROUPS, rows, cols), kind),
        dma((14,)),
        dma((3,)),
        dma((count,)),
        dma((count, 6)),
        dma((count, 6)),
        dma((count, 3)),
        dma((count, 3)),
        dma((count, 7)),
        dma((count, 7)),
        dma((count, SIDE)),
        dma((count, SIDE)),
        dma((2,)),
        dma((2,)),
    ]
    return pl.pallas_call(
        fused_kernel,
        out_shape=(
            jax.ShapeDtypeStruct(fields.shape, kind),
            jax.ShapeDtypeStruct((count, SIDE - 1, 2 * SIDE, SIDE * PICKS, rows, cols), kind),
            jax.ShapeDtypeStruct((PEERS, PICKS, PEERS), jnp.int32),
        ),
        in_specs=[pl.BlockSpec(memory_space=pltpu.SMEM), any_spec, any_spec, any_spec],
        out_specs=(any_spec, any_spec, any_spec),
        scratch_shapes=scratch,
        compiler_params=pltpu.CompilerParams(
            collective_id=0, has_side_effects=True, vmem_limit_bytes=62 * 1024 * 1024
        ),
    )(picks, wants, fields, weights)[0]


def tables(departures, blocks):
    me = lax.axis_index("region")
    flat = departures.reshape(-1)
    owner = flat // blocks
    local = flat % blocks
    key = jnp.arange(flat.shape[0], dtype=jnp.int32) * 64 + local
    named = owner[None, :] == jnp.arange(PEERS, dtype=jnp.int32)[:, None]
    first = jnp.min(jnp.where(named, key[None, :], 1 << 30), axis=1)
    last = jnp.max(jnp.where(named, key[None, :], 0), axis=1)
    wants = jnp.stack([jnp.where(first < (1 << 30), first, 0) % 64, last % 64], axis=0)
    is_first = jnp.any(named & (key[None, :] == first[:, None]), axis=0)
    rank = jnp.where(is_first, 0, 1)
    there, here = coords(owner), coords(me)
    away = [(there[i] - here[i]) % SIDE for i in range(3)]
    flip = (there[3] - here[3]) % 2
    picks = []
    for group in range(GROUPS):
        ja, jb, jc = (away[axis] for axis in axes_of(group))
        spot = (((jb * SIDE + jc) * 2 + flip) * SIDE + ja) * PICKS + rank
        picks.append(jnp.where(owner == me, REMOTE + local, spot))
    return wants, jnp.stack(picks).reshape((GROUPS,) + departures.shape)


def on_device(fields, weights, departures):
    blocks, field_count, levels, cols = fields.shape
    grouped = fields.reshape(blocks, GROUPS, field_count // GROUPS * levels, cols)
    wants, picks = tables(departures, blocks)
    return fused(picks, wants, grouped, weights).reshape(fields.shape)


def solution(mesh):
    in_specs = (P("region", None, None, None), P("region", None, None, None), P("region", None))
    out_specs = P("region", None, None, None)
    return jax.shard_map(on_device, mesh=mesh, in_specs=in_specs, out_specs=out_specs, check_vma=False)
```

time: 352 us -> 283 us (0.80)
  blocking collectives: 38.7 us -> 0 us
  Pallas kernels: 310 us -> 274 us
  local copies, waits for them, and re-layouts: 2.04 us -> 7.07 us
    all_gather x1 -> x0, blocking collectives: 38.7 us -> none  [on_device(): wants = lax.all_gather(wants.reshape(-1), 'region', axis=0)]
    pallas_call x2 -> x1, Pallas kernels: 310 us -> 274 us  [fused(): pl.pallas_call(fused_kernel, out_shape=(jax.ShapeDtypeStruct(fields.shape...]
    unnamed x3 -> x2, local copies, waits for them, and re-layouts: 1.57 us -> 6.71 us
where the time goes in v2:
time: 283 us; the launch traced here: 282 us
  Pallas kernels  274 us (97%)
  local copies, waits for them, and re-layouts  7.07 us (2%)
    pallas_call x1, Pallas kernels, fused(): pl.pallas_call(fused_kernel, out_shape=(jax.ShapeDtypeStruct(fields.shape...  274 us
    unnamed x2, local copies, waits for them, and re-layouts  6.71 us

profile of v2, /device:TPU:1, one launch (start us, length us, event | category | flops | bytes accessed | tf_op | source)
XLA Modules:
  0.0 282.4 jit_solution(1576303177900196312)
XLA Ops:
  0.0 0.8 copy.17
  0.8 0.1 ne.353
  0.9 0.1 div.91
  1.0 0.1 rem.373
  1.1 0.1 select_reduce_fusion
  1.2 0.1 fusion.1
  1.4 0.6 pad_add_fusion.1.own_wants
  1.9 0.1 select_n.271
  2.0 0.2 select_bitcast_fusion.2
  2.2 0.6 pad_add_fusion.picks
  2.8 273.6 %shard_map.37 = (bf16[48,3,128,128]{3,2,1,0:T(8,128)(2,1)}, bf16[6,3,8,8,64,128]{5,4,3,2,1,0:T(8,128)(2,1)}, s32[128,2,128]{2,1,0:T(2,128)}) custom-call(s32[3,48,8]{2,1,0:T(8,128)} %pad_add_fusion.picks, s32[2,128]{1,0:T(2,128)} %pad_add_fusion.1.own_wants, bf16[48,3,128,128]{3,2,1,0:T(8,128)(2,1)} %bitcast.13, bf16[48,8,128,128]{3,2,1,0:T(8,128)(2,1)} %weights.1), custom_call_target="tpu_custom_call" | custom-call | tf_op jit(solution)/shard_map/pallas_call | solution.py:337
  276.4 5.9 %copy.21 = bf16[48,12,32,128]{3,2,1,0:T(8,128)(2,1)} copy(bf16[48,12,32,128]{3,2,1,0:T(8,128)(2,1)} %bitcast.12) | data formatting | bytes 9437184
  (5 shorter events, 0.0 us)

commit v3 on v2

--- a/solution.py
+++ b/solution.py
@@ -9,10 +9,12 @@
 SIDE = 4
 PEERS = 128
 GROUPS = 3
-PHASES = 2
+PHASES = 4
+BUNDLES = 2
 PICKS = 2
 REMOTE = PEERS * PICKS
-CHUNK = 4
+CHUNK = 6
+SLOTS = 4
 
 
 def coords(device):
@@ -40,7 +42,7 @@
     count = GROUPS * PHASES
     near = [scratch[i * SIDE : (i + 1) * SIDE] for i in range(count)]
     scratch = scratch[count * SIDE :]
-    bundle, scratch = scratch[:GROUPS], scratch[GROUPS:]
+    bundle, scratch = scratch[: GROUPS * BUNDLES], scratch[GROUPS * BUNDLES :]
     pool, scratch = scratch[:count], scratch[count:]
     wants, tiles, result, *sems = scratch
     meta_send, meta_recv, own_sem, a_send, a_recv, b_send, b_recv, c_first, c_send, c_recv, keep_sem, w_sem, o_sem = sems
@@ -49,6 +51,9 @@
     rows = group_rows // PHASES
     here = coords(lax.axis_index("region"))
 
+    def bundle_of(k):
+        return bundle[k % (GROUPS * BUNDLES)]
+
     def send(src, dst, send_sem, recv_sem, device):
         copy = pltpu.make_async_remote_copy(
             src_ref=src, dst_ref=dst, send_sem=send_sem, recv_sem=recv_sem, device_id=(device,), device_id_type=MESH
@@ -67,7 +72,8 @@
     def fetch_tiles(chunk, slot):
         return keep(weights.at[pl.ds(chunk * CHUNK, CHUNK)], tiles.at[slot], w_sem.at[slot])
 
-    fetch_tiles(0, 0)
+    for step in range(SLOTS - 1):
+        fetch_tiles(step, step)
     own_copies = [
         keep(fields.at[:, k % GROUPS, pl.ds(k // GROUPS * rows, rows), :], near[k][0], own_sem.at[k])
         for k in range(count)
@@ -130,7 +136,7 @@
         copies[1].wait_recv()
         copies.append(send(near[k][1].at[high], near[k][2].at[high], a_send.at[k, 5], a_recv.at[k, 5], down))
 
-    def pick(k, ja, tb):
+    def pick(k, ja, tbs):
         group = k % GROUPS
         axis_a, axis_b, axis_c = axes_of(group)
         source = list(here)
@@ -138,12 +144,13 @@
         column = index_of(source)
 
         def one(t, carry):
-            away = [0, 0, 0]
-            away[axis_b] = tb
-            away[axis_c] = t // 2
-            row = ((away[0] * 4 + away[2]) * 4 + away[1]) * 2 + t % 2
-            for r in range(PICKS):
-                bundle[group][tb, t, ja * PICKS + r] = near[k][ja][wants[row, r, column]]
+            for tb in tbs:
+                away = [0, 0, 0]
+                away[axis_b] = tb
+                away[axis_c] = t // 2
+                row = ((away[0] * 4 + away[2]) * 4 + away[1]) * 2 + t % 2
+                for r in range(PICKS):
+                    bundle_of(k)[tb, t, ja * PICKS + r] = near[k][ja][wants[row, r, column]]
             return carry
 
         lax.fori_loop(0, 2 * SIDE, one, 0)
@@ -152,7 +159,7 @@
         jb = SIDE - tb
         _, axis_b, _ = axes_of(k % GROUPS)
         return send(
-            bundle[k % GROUPS].at[tb],
+            bundle_of(k).at[tb],
             landing.at[k, jb - 1],
             b_send.at[k, tb - 1],
             b_recv.at[k, jb - 1],
@@ -160,11 +167,10 @@
         )
 
     def send_on(k, jb):
-        group = k % GROUPS
-        _, _, axis_c = axes_of(group)
+        _, _, axis_c = axes_of(k % GROUPS)
         for t in (4, 5, 2, 3, 6, 7, 1, 0):
             tc, flip = divmod(t, 2)
-            src = bundle[group].at[0, t] if jb == 0 else landing.at[k, jb - 1, t]
+            src = bundle_of(k).at[0, t] if jb == 0 else landing.at[k, jb - 1, t]
             jc = (SIDE - tc) % SIDE
             dst = pool[k].at[pl.ds(((jb * SIDE + jc) * 2 + flip) * 8, 8)]
             if t == 0:
@@ -209,11 +215,12 @@
 
         def one(chunk, carry):
             slot = chunk % 2
-            await_bytes(tiles.at[slot], w_sem.at[slot])
-
-            @pl.when(chunk + 1 < chunks)
+            now, later = chunk % SLOTS, chunk + SLOTS - 1
+            await_bytes(tiles.at[now], w_sem.at[now])
+
+            @pl.when(later < chunks)
             def _():
-                fetch_tiles(chunk + 1, 1 - slot)
+                fetch_tiles(later, later % SLOTS)
 
             @pl.when(chunk >= 2)
             def _():
@@ -224,7 +231,7 @@
                 total = None
                 for s in range(0, weights.shape[1], 2):
                     left = jnp.concatenate([source(b, s), source(b, s + 1)], axis=1)
-                    right = tiles[slot, i, s : s + 2].reshape(2 * weights.shape[2], weights.shape[3])
+                    right = tiles[now, i, s : s + 2].reshape(2 * weights.shape[2], weights.shape[3])
                     dot = jnp.dot(left, right, preferred_element_type=jnp.float32)
                     total = dot if total is None else total + dot
                 total = total.astype(out.dtype)
@@ -237,65 +244,82 @@
         for chunk in (chunks - 2, chunks - 1):
             write_back(chunk, chunk % 2).wait()
 
+    def groups_of(phase):
+        return range(phase * GROUPS, (phase + 1) * GROUPS)
+
+    def start_phase(phase):
+        if phase < PHASES:
+            for k in groups_of(phase):
+                gathered[k] = start_gather(k)
+
+    def relay_phase(phase):
+        if phase < PHASES:
+            for k in groups_of(phase):
+                relay_gather(k, gathered[k])
+
+    def pick_phase(phase):
+        ks = groups_of(phase)
+        every = range(SIDE)
+        for k in ks:
+            if phase >= BUNDLES:
+                before = k - GROUPS * BUNDLES
+                free_bundle(before, along[before])
+            pick(k, 0, every)
+        for k in ks:
+            gathered[k][3].wait_recv()
+            pick(k, 1, every)
+            gathered[k][2].wait_recv()
+            pick(k, 3, every)
+        for k in ks:
+            along[k] = {}
+            gathered[k][4].wait_recv()
+            gathered[k][5].wait_recv()
+            for tb in (2, 1, 3, 0):
+                pick(k, 2, (tb,))
+                if tb:
+                    along[k][SIDE - tb] = send_bundle(k, tb)
+            send_on(k, 0)
+
+    def forward_phase(phase):
+        for jb in (1, 3, 2):
+            for k in groups_of(phase):
+                along[k][jb].wait_recv()
+                send_on(k, jb)
+
+    def finish_phase(phase):
+        if phase:
+            for step in range(SLOTS - 1):
+                fetch_tiles(step, step)
+        for k in groups_of(phase):
+            await_pool(k)
+            if phase >= PHASES - BUNDLES:
+                free_bundle(k, along[k])
+        interpolate(phase)
+
     gathered, along = {}, {}
     meta = send_wants_z()
-    for k in range(GROUPS):
-        gathered[k] = start_gather(k)
+    start_phase(0)
     own_row.wait()
     await_bytes(want_rows.at[pl.ds(0, 7)], meta_recv.at[0])
     meta += send_wants(2, 7, 8, 1)
-    for k in range(GROUPS):
-        relay_gather(k, gathered[k])
+    relay_phase(0)
     await_bytes(want_rows.at[pl.ds(0, 24)], meta_recv.at[1])
     meta += send_wants(0, 10, 32, 2)
+    start_phase(1)
     for copy in own_copies:
         copy.wait()
     await_bytes(want_rows.at[pl.ds(0, 96)], meta_recv.at[2])
-    table = keep(want_rows, wants, meta_send.at[13])
-    table.wait()
-
-    for phase in range(PHASES):
-        ks = range(phase * GROUPS, (phase + 1) * GROUPS)
-        for k in ks:
-            if phase:
-                free_bundle(k - GROUPS, along[k - GROUPS])
-            for tb in range(SIDE):
-                pick(k, 0, tb)
-        for k in ks:
-            gathered[k][3].wait_recv()
-            for tb in range(SIDE):
-                pick(k, 1, tb)
-            gathered[k][2].wait_recv()
-            for tb in range(SIDE):
-                pick(k, 3, tb)
-        for k in ks:
-            gathered[k][4].wait_recv()
-            gathered[k][5].wait_recv()
-            if phase + 1 < PHASES:
-                gathered[k + GROUPS] = start_gather(k + GROUPS)
-        for k in ks:
-            along[k] = {}
-            for tb in (2, 1, 3, 0):
-                pick(k, 2, tb)
-                if tb:
-                    along[k][SIDE - tb] = send_bundle(k, tb)
-            send_on(k, 0)
-        if phase + 1 < PHASES:
-            for k in ks:
-                relay_gather(k + GROUPS, gathered[k + GROUPS])
-        for jb in (1, 3, 2):
-            for k in ks:
-                along[k][jb].wait_recv()
-                send_on(k, jb)
-
-    for phase in range(PHASES):
-        for k in range(phase * GROUPS, (phase + 1) * GROUPS):
-            await_pool(k)
-            if phase == PHASES - 1:
-                free_bundle(k, along[k])
-        if phase:
-            fetch_tiles(0, 0)
-        interpolate(phase)
+    keep(want_rows, wants, meta_send.at[13]).wait()
+
+    for step in range(PHASES + 2):
+        if step < PHASES:
+            pick_phase(step)
+            relay_phase(step + 1)
+            start_phase(step + 2)
+        if 1 <= step <= PHASES:
+            forward_phase(step - 1)
+        if step >= 2:
+            finish_phase(step - 2)
 
     for copy in meta:
         copy.wait_send()
@@ -314,11 +338,11 @@
     dma = pltpu.SemaphoreType.DMA
     any_spec = pl.BlockSpec(memory_space=pl.ANY)
     scratch = [pltpu.VMEM((blocks, rows, cols), kind) for _ in range(count * SIDE)]
-    scratch += [pltpu.VMEM((SIDE, 2 * SIDE, SIDE * PICKS, rows, cols), kind) for _ in range(GROUPS)]
+    scratch += [pltpu.VMEM((SIDE, 2 * SIDE, SIDE * PICKS, rows, cols), kind) for _ in range(GROUPS * BUNDLES)]
     scratch += [pltpu.VMEM((REMOTE, rows, cols), kind) for _ in range(count)]
     scratch += [
         pltpu.SMEM((PEERS, PICKS, PEERS), jnp.int32),
-        pltpu.VMEM((2, CHUNK) + weights.shape[1:], kind),
+        pltpu.VMEM((SLOTS, CHUNK) + weights.shape[1:], kind),
         pltpu.VMEM((2, CHUNK, GROUPS, rows, cols), kind),
         dma((14,)),
         dma((3,)),
@@ -331,7 +355,7 @@
         dma((count, 7)),
         dma((count, SIDE)),
         dma((count, SIDE)),
-        dma((2,)),
+        dma((SLOTS,)),
         dma((2,)),
     ]
     return pl.pallas_call(

time: 283 us -> 263 us (0.929)
  Pallas kernels: 274 us -> 254 us
    pallas_call x1, Pallas kernels: 274 us -> 254 us  [fused(): pl.pallas_call(fused_kernel, out_shape=(jax.ShapeDtypeStruct(fields.shape...]
where the time goes in v3:
time: 263 us
  Pallas kernels  254 us (97%)
  local copies, waits for them, and re-layouts  7.07 us (3%)
    pallas_call x1, Pallas kernels, fused(): pl.pallas_call(fused_kernel, out_shape=(jax.ShapeDtypeStruct(fields.shape...  254 us
    unnamed x2, local copies, waits for them, and re-layouts  6.71 us

profile of v3, /device:TPU:1, one launch (start us, length us, event | category | flops | bytes accessed | tf_op | source)
XLA Modules:
  0.0 263.2 jit_solution(553296900527167977)
XLA Ops:
  0.0 0.8 copy.17
  0.8 0.1 ne.353
  0.9 0.1 div.91
  1.0 0.1 rem.373
  1.1 0.1 select_reduce_fusion
  1.2 0.1 fusion.1
  1.4 0.6 pad_add_fusion.1.own_wants
  1.9 0.1 select_n.271
  2.0 0.2 select_bitcast_fusion.2
  2.2 0.6 pad_add_fusion.picks
  2.8 254.4 %shard_map.37 = (bf16[48,3,128,128]{3,2,1,0:T(8,128)(2,1)}, bf16[12,3,8,8,32,128]{5,4,3,2,1,0:T(8,128)(2,1)}, s32[128,2,128]{2,1,0:T(2,128)}) custom-call(s32[3,48,8]{2,1,0:T(8,128)} %pad_add_fusion.picks, s32[2,128]{1,0:T(2,128)} %pad_add_fusion.1.own_wants, bf16[48,3,128,128]{3,2,1,0:T(8,128)(2,1)} %bitcast.13, bf16[48,8,128,128]{3,2,1,0:T(8,128)(2,1)} %weights.1), custom_call_target="tpu_custom_call" | custom-call | tf_op jit(solution)/shard_map/pallas_call | solution.py:361
  257.2 5.9 %copy.21 = bf16[48,12,32,128]{3,2,1,0:T(8,128)(2,1)} copy(bf16[48,12,32,128]{3,2,1,0:T(8,128)(2,1)} %bitcast.12) | data formatting | bytes 9437184
  (5 shorter events, 0.0 us)

commit v4 on v3

--- a/solution.py
+++ b/solution.py
@@ -14,6 +14,7 @@
 PICKS = 2
 REMOTE = PEERS * PICKS
 CHUNK = 6
+STORES = 8
 SLOTS = 4
 
 
@@ -38,13 +39,13 @@
     return group, (group + 1) % 3, (group + 2) % 3
 
 
-def fused_kernel(picks, own_wants, fields, weights, out, landing, want_rows, *scratch):
+def fused_kernel(departures, fields, weights, out, landing, want_rows, *scratch):
     count = GROUPS * PHASES
     near = [scratch[i * SIDE : (i + 1) * SIDE] for i in range(count)]
     scratch = scratch[count * SIDE :]
     bundle, scratch = scratch[: GROUPS * BUNDLES], scratch[GROUPS * BUNDLES :]
     pool, scratch = scratch[:count], scratch[count:]
-    wants, tiles, result, *sems = scratch
+    wants, picks, own_wants, spots, tiles, result, *sems = scratch
     meta_send, meta_recv, own_sem, a_send, a_recv, b_send, b_recv, c_first, c_send, c_recv, keep_sem, w_sem, o_sem = sems
     blocks, _, group_rows, _ = fields.shape
     half = blocks // 2
@@ -78,13 +79,62 @@
         keep(fields.at[:, k % GROUPS, pl.ds(k // GROUPS * rows, rows), :], near[k][0], own_sem.at[k])
         for k in range(count)
     ]
-    own_row = keep(own_wants, want_rows.at[0], meta_send.at[13])
 
     peers = [shifted(here, axis, steps, flip) for axis in range(3) for steps in (1, 2, 3) for flip in (0, 1)]
     peers.append(shifted(here, 0, 0, 1))
     barrier = pltpu.get_barrier_semaphore()
     for peer in peers:
         pl.semaphore_signal(barrier, inc=1, device_id=(peer,), device_id_type=MESH)
+
+    def tables():
+        ids = departures[...]
+        slots = ids.shape[1]
+        lane = lax.broadcasted_iota(jnp.int32, (blocks, PEERS), 1)
+        block = lax.broadcasted_iota(jnp.int32, (blocks, PEERS), 0)
+
+        def spread(columns):
+            wide = jnp.zeros((blocks, PEERS), jnp.int32)
+            for s, column in enumerate(columns):
+                wide = jnp.where(lane % slots == s, column, wide)
+            return wide
+
+        owner = (ids * 43691) >> 21
+        local = ids - owner * blocks
+        keys, named = [], []
+        first = jnp.full((blocks, PEERS), 1 << 30, jnp.int32)
+        last = jnp.zeros((blocks, PEERS), jnp.int32)
+        for s in range(slots):
+            key = (block * slots + s) * 64 + local[:, s : s + 1]
+            keys.append(key)
+            named.append(owner[:, s : s + 1] == lane)
+            first = jnp.minimum(first, jnp.where(named[s], key, 1 << 30))
+            last = jnp.maximum(last, jnp.where(named[s], key, 0))
+        first = jnp.min(first, axis=0, keepdims=True)
+        last = jnp.max(last, axis=0, keepdims=True)
+        own_wants[0:1] = first % 64
+        own_wants[1:2] = last % 64
+        ranks = []
+        for s in range(slots):
+            later = jnp.where(named[s], jnp.where(keys[s] == first, 0, 1), 0)
+            ranks.append(jnp.max(later, axis=1, keepdims=True))
+        rank = spread(ranks)
+        owner = spread([owner[:, s : s + 1] for s in range(slots)])
+        local = spread([local[:, s : s + 1] for s in range(slots)])
+        there = (owner >> 5, (owner >> 3) & 3, (owner >> 1) & 3)
+        away = [(there[i] - here[i]) & 3 for i in range(3)]
+        flip = (owner - here[3]) & 1
+        group = lane // slots
+
+        def along_axis(which):
+            a, b, c = (axes_of(g)[which] for g in range(GROUPS))
+            return jnp.where(group == 0, away[a], jnp.where(group == 1, away[b], away[c]))
+
+        spot = (((along_axis(1) * SIDE + along_axis(2)) * 2 + flip) * SIDE + along_axis(0)) * PICKS + rank
+        spots[...] = jnp.where(owner == lax.axis_index("region"), REMOTE + local, spot)
+
+    tables()
+    own_row = keep(own_wants, want_rows.at[0], meta_send.at[13])
+    pick_table = keep(spots, picks, meta_send.at[14])
     pl.semaphore_wait(barrier, len(peers))
 
     def send_wants_z():
@@ -207,7 +257,7 @@
             parts = []
             for group in range(GROUPS):
                 k = phase * GROUPS + group
-                at = picks[group, b, s]
+                at = picks[b, group * weights.shape[1] + s]
                 away = pool[k][jnp.minimum(at, REMOTE - 1)]
                 local = near[k][0][jnp.maximum(at - REMOTE, 0)]
                 parts.append(jnp.where(at < REMOTE, away, local))
@@ -300,6 +350,7 @@
     meta = send_wants_z()
     start_phase(0)
     own_row.wait()
+    pick_table.wait()
     await_bytes(want_rows.at[pl.ds(0, 7)], meta_recv.at[0])
     meta += send_wants(2, 7, 8, 1)
     relay_phase(0)
@@ -330,7 +381,7 @@
             await_bytes(pool[k].at[pl.ds(0, 24)], c_send.at[k, t - 1])
 
 
-def fused(picks, wants, fields, weights):
+def fused(departures, fields, weights):
     blocks, _, group_rows, cols = fields.shape
     rows = group_rows // PHASES
     count = GROUPS * PHASES
@@ -342,9 +393,12 @@
     scratch += [pltpu.VMEM((REMOTE, rows, cols), kind) for _ in range(count)]
     scratch += [
         pltpu.SMEM((PEERS, PICKS, PEERS), jnp.int32),
+        pltpu.SMEM((blocks, PEERS), jnp.int32),
+        pltpu.VMEM((PICKS, PEERS), jnp.int32),
+        pltpu.VMEM((blocks, PEERS), jnp.int32),
         pltpu.VMEM((SLOTS, CHUNK) + weights.shape[1:], kind),
         pltpu.VMEM((2, CHUNK, GROUPS, rows, cols), kind),
-        dma((14,)),
+        dma((15,)),
         dma((3,)),
         dma((count,)),
         dma((count, 6)),
@@ -365,43 +419,49 @@
             jax.ShapeDtypeStruct((count, SIDE - 1, 2 * SIDE, SIDE * PICKS, rows, cols), kind),
             jax.ShapeDtypeStruct((PEERS, PICKS, PEERS), jnp.int32),
         ),
-        in_specs=[pl.BlockSpec(memory_space=pltpu.SMEM), any_spec, any_spec, any_spec],
+        in_specs=[pl.BlockSpec(memory_space=pltpu.VMEM), any_spec, any_spec],
         out_specs=(any_spec, any_spec, any_spec),
         scratch_shapes=scratch,
         compiler_params=pltpu.CompilerParams(
             collective_id=0, has_side_effects=True, vmem_limit_bytes=62 * 1024 * 1024
         ),
-    )(picks, wants, fields, weights)[0]
-
-
-def tables(departures, blocks):
-    me = lax.axis_index("region")
-    flat = departures.reshape(-1)
-    owner = flat // blocks
-    local = flat % blocks
-    key = jnp.arange(flat.shape[0], dtype=jnp.int32) * 64 + local
-    named = owner[None, :] == jnp.arange(PEERS, dtype=jnp.int32)[:, None]
-    first = jnp.min(jnp.where(named, key[None, :], 1 << 30), axis=1)
-    last = jnp.max(jnp.where(named, key[None, :], 0), axis=1)
-    wants = jnp.stack([jnp.where(first < (1 << 30), first, 0) % 64, last % 64], axis=0)
-    is_first = jnp.any(named & (key[None, :] == first[:, None]), axis=0)
-    rank = jnp.where(is_first, 0, 1)
-    there, here = coords(owner), coords(me)
-    away = [(there[i] - here[i]) % SIDE for i in range(3)]
-    flip = (there[3] - here[3]) % 2
-    picks = []
-    for group in range(GROUPS):
-        ja, jb, jc = (away[axis] for axis in axes_of(group))
-        spot = (((jb * SIDE + jc) * 2 + flip) * SIDE + ja) * PICKS + rank
-        picks.append(jnp.where(owner == me, REMOTE + local, spot))
-    return wants, jnp.stack(picks).reshape((GROUPS,) + departures.shape)
+    )(departures, fields, weights)[0]
+
+
+def store_kernel(src, dst, held, in_sems, out_sems):
+    step = src.shape[0] // STORES
+    spans = [pl.ds(i * step, step) for i in range(STORES)]
+    loads = [pltpu.make_async_copy(src.at[span], held.at[span], in_sems.at[i]) for i, span in enumerate(spans)]
+    stores = [pltpu.make_async_copy(held.at[span], dst.at[span], out_sems.at[i]) for i, span in enumerate(spans)]
+    for copy in loads:
+        copy.start()
+    for i in range(STORES):
+        loads[i].wait()
+        stores[i].start()
+    for copy in stores:
+        copy.wait()
+
+
+def store(result):
+    any_spec = pl.BlockSpec(memory_space=pl.ANY)
+    return pl.pallas_call(
+        store_kernel,
+        out_shape=jax.ShapeDtypeStruct(result.shape, result.dtype),
+        in_specs=[any_spec],
+        out_specs=any_spec,
+        scratch_shapes=[
+            pltpu.VMEM(result.shape, result.dtype),
+            pltpu.SemaphoreType.DMA((STORES,)),
+            pltpu.SemaphoreType.DMA((STORES,)),
+        ],
+        compiler_params=pltpu.CompilerParams(vmem_limit_bytes=60 * 1024 * 1024),
+    )(result)
 
 
 def on_device(fields, weights, departures):
     blocks, field_count, levels, cols = fields.shape
     grouped = fields.reshape(blocks, GROUPS, field_count // GROUPS * levels, cols)
-    wants, picks = tables(departures, blocks)
-    return fused(picks, wants, grouped, weights).reshape(fields.shape)
+    return store(fused(departures, grouped, weights)).reshape(fields.shape)
 
 
 def solution(mesh):

time: 263 us -> 259 us (0.985)
  local copies, waits for them, and re-layouts: 7.07 us -> 1.37 us
  Pallas kernels: 254 us -> 257 us
    unnamed x2 -> x1, local copies, waits for them, and re-layouts: 6.71 us -> 1.37 us
    pallas_call x0 -> x1, Pallas kernels: none -> 4.12 us  [store(): pl.pallas_call(store_kernel, out_shape=jax.ShapeDtypeStruct(result.shape,...]
where the time goes in v4:
time: 259 us
  Pallas kernels  257 us (99%)
    pallas_call x1, Pallas kernels, fused(): pl.pallas_call(fused_kernel, out_shape=(jax.ShapeDtypeStruct(fields.shape...  253 us

profile of v4, /device:TPU:1, one launch (start us, length us, event | category | flops | bytes accessed | tf_op | source)
XLA Modules:
  0.0 258.8 jit_solution(4638886378562833052)
XLA Ops:
  0.0 1.4 copy.4.departures
  1.4 253.3 %shard_map.37 = (bf16[48,3,128,128]{3,2,1,0:T(8,128)(2,1)}, bf16[12,3,8,8,32,128]{5,4,3,2,1,0:T(8,128)(2,1)}, s32[128,2,128]{2,1,0:T(2,128)}) custom-call(s32[48,8]{1,0:T(8,128)} %copy.4.departures, bf16[48,3,128,128]{3,2,1,0:T(8,128)(2,1)} %bitcast.2, bf16[48,8,128,128]{3,2,1,0:T(8,128)(2,1)} %weights.1), custom_call_target="tpu_custom_call" | custom-call | tf_op jit(solution)/shard_map/pallas_call | solution.py:415
  254.6 4.1 %shard_map.38 = bf16[48,3,128,128]{3,2,1,0:T(8,128)(2,1)} custom-call(bf16[48,3,128,128]{3,2,1,0:T(8,128)(2,1)} %get-tuple-element.6.src), custom_call_target="tpu_custom_call" | custom-call | tf_op jit(solution)/shard_map/pallas_call | solution.py:447

commit v5 on v4

--- a/solution.py
+++ b/solution.py
@@ -14,7 +14,7 @@
 PICKS = 2
 REMOTE = PEERS * PICKS
 CHUNK = 6
-STORES = 8
+STORES = 4
 SLOTS = 4
 
 
@@ -39,13 +39,13 @@
     return group, (group + 1) % 3, (group + 2) % 3
 
 
-def fused_kernel(departures, fields, weights, out, landing, want_rows, *scratch):
+def fused_kernel(departures_home, fields, weights, out, landing, want_rows, *scratch):
     count = GROUPS * PHASES
     near = [scratch[i * SIDE : (i + 1) * SIDE] for i in range(count)]
     scratch = scratch[count * SIDE :]
     bundle, scratch = scratch[: GROUPS * BUNDLES], scratch[GROUPS * BUNDLES :]
     pool, scratch = scratch[:count], scratch[count:]
-    wants, picks, own_wants, spots, tiles, result, *sems = scratch
+    wants, picks, own_wants, spots, departures, tiles, result, *sems = scratch
     meta_send, meta_recv, own_sem, a_send, a_recv, b_send, b_recv, c_first, c_send, c_recv, keep_sem, w_sem, o_sem = sems
     blocks, _, group_rows, _ = fields.shape
     half = blocks // 2
@@ -73,6 +73,7 @@
     def fetch_tiles(chunk, slot):
         return keep(weights.at[pl.ds(chunk * CHUNK, CHUNK)], tiles.at[slot], w_sem.at[slot])
 
+    ids_copy = keep(departures_home, departures, meta_send.at[14])
     for step in range(SLOTS - 1):
         fetch_tiles(step, step)
     own_copies = [
@@ -132,6 +133,7 @@
         spot = (((along_axis(1) * SIDE + along_axis(2)) * 2 + flip) * SIDE + along_axis(0)) * PICKS + rank
         spots[...] = jnp.where(owner == lax.axis_index("region"), REMOTE + local, spot)
 
+    ids_copy.wait()
     tables()
     own_row = keep(own_wants, want_rows.at[0], meta_send.at[13])
     pick_table = keep(spots, picks, meta_send.at[14])
@@ -396,6 +398,7 @@
         pltpu.SMEM((blocks, PEERS), jnp.int32),
         pltpu.VMEM((PICKS, PEERS), jnp.int32),
         pltpu.VMEM((blocks, PEERS), jnp.int32),
+        pltpu.VMEM(departures.shape, jnp.int32),
         pltpu.VMEM((SLOTS, CHUNK) + weights.shape[1:], kind),
         pltpu.VMEM((2, CHUNK, GROUPS, rows, cols), kind),
         dma((15,)),
@@ -419,7 +422,7 @@
             jax.ShapeDtypeStruct((count, SIDE - 1, 2 * SIDE, SIDE * PICKS, rows, cols), kind),
             jax.ShapeDtypeStruct((PEERS, PICKS, PEERS), jnp.int32),
         ),
-        in_specs=[pl.BlockSpec(memory_space=pltpu.VMEM), any_spec, any_spec],
+        in_specs=[any_spec, any_spec, any_spec],
         out_specs=(any_spec, any_spec, any_spec),
         scratch_shapes=scratch,
         compiler_params=pltpu.CompilerParams(

time: 259 us -> 258 us (level)
  no operation moved by 1% of the time
where the time goes in v5:
time: 258 us
  Pallas kernels  256 us (99%)
    pallas_call x1, Pallas kernels, fused(): pl.pallas_call(fused_kernel, out_shape=(jax.ShapeDtypeStruct(fields.shape...  253 us

profile of v5, /device:TPU:1, one launch (start us, length us, event | category | flops | bytes accessed | tf_op | source)
XLA Modules:
  0.0 257.7 jit_solution(12760005750831744314)
XLA Ops:
  0.0 1.4 copy.4.departures_home
  1.4 252.6 %shard_map.37 = (bf16[48,3,128,128]{3,2,1,0:T(8,128)(2,1)}, bf16[12,3,8,8,32,128]{5,4,3,2,1,0:T(8,128)(2,1)}, s32[128,2,128]{2,1,0:T(2,128)}) custom-call(s32[48,8]{1,0:T(8,128)} %copy.4.departures_home, bf16[48,3,128,128]{3,2,1,0:T(8,128)(2,1)} %bitcast.2, bf16[48,8,128,128]{3,2,1,0:T(8,128)(2,1)} %weights.1), custom_call_target="tpu_custom_call" | custom-call | tf_op jit(solution)/shard_map/pallas_call | solution.py:418
  254.0 3.8 %shard_map.38 = bf16[48,3,128,128]{3,2,1,0:T(8,128)(2,1)} custom-call(bf16[48,3,128,128]{3,2,1,0:T(8,128)(2,1)} %get-tuple-element.6.src), custom_call_target="tpu_custom_call" | custom-call | tf_op jit(solution)/shard_map/pallas_call | solution.py:450

commit v6 on v5

--- a/solution.py
+++ b/solution.py
@@ -366,9 +366,9 @@
 
     for step in range(PHASES + 2):
         if step < PHASES:
-            pick_phase(step)
             relay_phase(step + 1)
             start_phase(step + 2)
+            pick_phase(step)
         if 1 <= step <= PHASES:
             forward_phase(step - 1)
         if step >= 2:

time: 258 us -> 258 us (level)
  no operation moved by 1% of the time
where the time goes in v6:
time: 258 us
  Pallas kernels  256 us (99%)
    pallas_call x1, Pallas kernels, fused(): pl.pallas_call(fused_kernel, out_shape=(jax.ShapeDtypeStruct(fields.shape...  252 us

profile of v6, /device:TPU:1, one launch (start us, length us, event | category | flops | bytes accessed | tf_op | source)
XLA Modules:
  0.0 257.6 jit_solution(14282387898649793501)
XLA Ops:
  0.0 1.4 copy.4.departures_home
  1.4 252.5 %shard_map.37 = (bf16[48,3,128,128]{3,2,1,0:T(8,128)(2,1)}, bf16[12,3,8,8,32,128]{5,4,3,2,1,0:T(8,128)(2,1)}, s32[128,2,128]{2,1,0:T(2,128)}) custom-call(s32[48,8]{1,0:T(8,128)} %copy.4.departures_home, bf16[48,3,128,128]{3,2,1,0:T(8,128)(2,1)} %bitcast.2, bf16[48,8,128,128]{3,2,1,0:T(8,128)(2,1)} %weights.1), custom_call_target="tpu_custom_call" | custom-call | tf_op jit(solution)/shard_map/pallas_call | solution.py:418
  253.8 3.8 %shard_map.38 = bf16[48,3,128,128]{3,2,1,0:T(8,128)(2,1)} custom-call(bf16[48,3,128,128]{3,2,1,0:T(8,128)(2,1)} %get-tuple-element.6.src), custom_call_target="tpu_custom_call" | custom-call | tf_op jit(solution)/shard_map/pallas_call | solution.py:450
